TPU v7x, 32 devices: a whole 2x2x4 slice. The times are simulated.
32 devices in a mesh: shot: 8 (over z, x), depth: 4 (over y, core).
Axes of the slice: x: 2, y: 2, z: 4, core: 2. Of those that a mesh axis runs over, the one named last changes fastest.
Arguments:
- prev_fields: float32 [8, 2, 32, 16, 128], P('shot', None, 'depth'), may hold values from -6 to 6
- cur_fields: float32 [8, 2, 32, 16, 128], P('shot', None, 'depth'), may hold values from -6 to 6
- speed_term: bfloat16 [8, 32, 16, 128], P('shot', 'depth'), may hold values from 0.039794922 to 0.119628906
- epsilon: bfloat16 [8, 32, 16, 128], P('shot', 'depth'), may hold values from 0 to 0.25
- tilt: bfloat16 [8, 32, 16, 128], P('shot', 'depth'), may hold values from 0 to 1.5
- azimuth: bfloat16 [8, 32, 16, 128], P('shot', 'depth'), may hold values from -3.140625 to 3.140625
- aperture_anchor: int32 [8], replicated, may hold values from -8 to 24
- slot_block: int32 [32], replicated, may hold values from 0 to 31, as said below
- band_width: int32 [32], replicated, may hold values from 1 to 4
- depth_damp: float32 [32], replicated, may hold values from 0.02 to 0.1
Outputs:
- gradient: float32 [32, 128, 32], P('shot', 'depth')
Inputs may be any that keep to these rules, and one draw needn't show every extreme that they name: Slots 4 * q to 4 * q + 3 hold the image blocks 2 r, 2 r + 1, 2 r + 16 and 2 r + 32 / 2 + 1 for some r, each r once, so that slot_block is a permutation of the blocks. `aperture_anchor`: every aperture covers at least 8 image blocks, and at most 2 of them held by one shot index; every aperture reaches 2 for some shot index.
All inputs are finite; a program needn't handle non-finite values.
Results may differ from a plain program's by a relative error of at most 0.0003.
Values may be sent and summed in bfloat16 or wider, within the bound.
A program may use at most 64 MiB of HBM per device.

v0:
```python
import jax
import jax.numpy as jnp
from jax import lax
from jax.sharding import PartitionSpec as P

NT = 8
IMB = 4
CAP = 2


def with_halo(cells, sides, width):
    for axis, dim in sides:
        count = lax.axis_size(axis)
        ends = count - 1
        head = lax.slice_in_dim(cells, 0, width, axis=dim)
        tail = lax.slice_in_dim(cells, cells.shape[dim] - width, cells.shape[dim], axis=dim)
        cells = jnp.concatenate(
            [
                lax.ppermute(tail, axis, [(i, (i + 1) % count) for i in range(ends)]),
                cells,
                lax.ppermute(head, axis, [((i + 1) % count, i) for i in range(ends)]),
            ],
            axis=dim,
        )
    return cells


def weights_of(speed_term, epsilon, tilt, azimuth):
    speed = speed_term.astype(jnp.float32)
    ratio = epsilon.astype(jnp.float32)
    theta = tilt.astype(jnp.float32)
    sweep = azimuth.astype(jnp.float32)
    sine = jnp.sin(theta)
    axis_z = jnp.cos(theta)
    axis_x = sine * jnp.cos(sweep)
    axis_y = sine * jnp.sin(sweep)
    iso_part = 1.0 + 2.0 * ratio
    anisotropy = -2.0 * ratio
    return (
        speed * (iso_part + anisotropy * axis_z * axis_z),
        speed * (iso_part + anisotropy * axis_x * axis_x),
        speed * (iso_part + anisotropy * axis_y * axis_y),
        speed * (2.0 * anisotropy * axis_z * axis_x),
        speed * (2.0 * anisotropy * axis_z * axis_y),
        speed * (2.0 * anisotropy * axis_x * axis_y),
    )


def apply_operator(extended, weights):
    leading = extended.ndim - 3
    padded = jnp.pad(extended, [(0, 0)] * leading + [(0, 0), (1, 1), (1, 1)])
    center = padded[..., 1:-1, 1:-1, 1:-1]
    along_z = padded[..., 2:, 1:-1, 1:-1] + padded[..., :-2, 1:-1, 1:-1] - 2.0 * center
    along_x = padded[..., 1:-1, 2:, 1:-1] + padded[..., 1:-1, :-2, 1:-1] - 2.0 * center
    along_y = padded[..., 1:-1, 1:-1, 2:] + padded[..., 1:-1, 1:-1, :-2] - 2.0 * center
    cross_zx = 0.25 * (
        padded[..., 2:, 2:, 1:-1]
        - padded[..., 2:, :-2, 1:-1]
        - padded[..., :-2, 2:, 1:-1]
        + padded[..., :-2, :-2, 1:-1]
    )
    cross_zy = 0.25 * (
        padded[..., 2:, 1:-1, 2:]
        - padded[..., 2:, 1:-1, :-2]
        - padded[..., :-2, 1:-1, 2:]
        + padded[..., :-2, 1:-1, :-2]
    )
    cross_xy = 0.25 * (
        padded[..., 1:-1, 2:, 2:]
        - padded[..., 1:-1, 2:, :-2]
        - padded[..., 1:-1, :-2, 2:]
        + padded[..., 1:-1, :-2, :-2]
    )
    return (
        weights[0] * along_z
        + weights[1] * along_x
        + weights[2] * along_y
        + weights[3] * cross_zx
        + weights[4] * cross_zy
        + weights[5] * cross_xy
    )


def band_matrix(band_width, depth_damp):
    length = band_width.shape[0]
    index = jnp.arange(length, dtype=jnp.int32)
    distance = jnp.abs(index[:, None] - index[None, :])
    reach = jnp.maximum(band_width[:, None], band_width[None, :])
    adjacent = ((distance > 0) & (distance <= reach)).astype(jnp.float32)
    return jnp.diag(depth_damp + jnp.sum(adjacent, axis=1)) - adjacent


def shards(
    prev_fields,
    cur_fields,
    speed_term,
    epsilon,
    tilt,
    azimuth,
    aperture_anchor,
    slot_block,
    band_width,
    depth_damp,
):
    earlier_field = prev_fields[0]
    current = cur_fields[0]
    picture = jnp.zeros(current.shape[1:], jnp.float32)
    weights = weights_of(speed_term[0], epsilon[0], tilt[0], azimuth[0])
    for counter in range(NT):
        extended = with_halo(current, (("depth", 1),), 1)
        following = 2.0 * current - earlier_field + apply_operator(extended, weights)
        picture = picture + following[0] * following[1]
        earlier_field, current = (current, following)
    picture = picture * (1.0 / NT)
    shots = lax.axis_size("shot")
    my_shot = lax.axis_index("shot")
    span = picture.shape[1]
    blocks = slot_block.shape[0]
    offsets = jnp.arange(span, dtype=jnp.int32)
    target = aperture_anchor[:, None] + offsets[None, :]
    inside = (target >= 0) & (target < blocks)
    slot_ids = jnp.arange(blocks, dtype=jnp.int32)
    matches = slot_block[None, None, :] == target[:, :, None]
    slot_index = jnp.sum(jnp.where(matches, slot_ids[None, None, :], 0), axis=2)
    holder = slot_index // IMB
    shot_ids = jnp.arange(shots, dtype=jnp.int32)
    mine = shot_ids == my_shot
    position = jnp.sum(jnp.where(matches, (slot_ids % IMB)[None, None, :], 0), axis=2)
    earlier_mask = offsets[:, None] < offsets[None, :]
    same_holder = (
        (holder[:, :, None] == holder[:, None, :]) & inside[:, :, None] & earlier_mask[None, :, :]
    )
    order_rank = jnp.sum(same_holder.astype(jnp.int32), axis=1)
    cap_ids = jnp.arange(CAP, dtype=jnp.int32)
    my_holder = jnp.sum(jnp.where(mine[:, None], holder, 0), axis=0)
    my_rank = jnp.sum(jnp.where(mine[:, None], order_rank, 0), axis=0)
    my_inside = jnp.any(inside & mine[:, None], axis=0)
    sender = (
        (shot_ids[:, None, None] == my_holder[None, None, :])
        & (cap_ids[None, :, None] == my_rank[None, None, :])
        & my_inside[None, None, :]
    ).astype(jnp.float32)
    parcels = jnp.einsum("qck,zky->qcyz", sender, picture, precision=lax.Precision.HIGHEST)
    arrived = lax.all_to_all(parcels, "shot", split_axis=0, concat_axis=0, tiled=True)
    local_ids = jnp.arange(IMB, dtype=jnp.int32)
    receiver = (
        (local_ids[:, None, None, None] == position[None, :, None, :])
        & (holder == my_shot)[None, :, None, :]
        & inside[None, :, None, :]
        & (cap_ids[None, None, :, None] == order_rank[None, :, None, :])
    ).astype(jnp.float32)
    collect = jnp.sum(receiver, axis=3)
    owned = jnp.einsum("jsc,scyz->jyz", collect, arrived, precision=lax.Precision.HIGHEST)
    traces = lax.all_to_all(owned, "depth", split_axis=1, concat_axis=2, tiled=True)
    depth_total = traces.shape[2]
    columns = traces.reshape(-1, depth_total)
    matrix = band_matrix(band_width, depth_damp)
    factor = jnp.linalg.cholesky(matrix)
    solved = jax.scipy.linalg.cho_solve((factor, True), columns.T)
    return solved.T.reshape(traces.shape)


def solution(mesh):
    placed = (
        P("shot", None, "depth", None, None),
        P("shot", None, "depth", None, None),
        P("shot", "depth", None, None),
        P("shot", "depth", None, None),
        P("shot", "depth", None, None),
        P("shot", "depth", None, None),
        P(),
        P(),
        P(),
        P(),
    )
    return jax.shard_map(
        shards, mesh=mesh, in_specs=placed, out_specs=P("shot", "depth", None), check_vma=False
    )
```

profile of v0, /device:TPU:0, one launch (start us, length us, event | category | flops | bytes accessed | tf_op | source)
XLA Modules:
  0.0 90.5 jit_solution(11167719824765274478)
XLA Ops:
  0.0 0.7 fusion.209
  0.7 1.3 %collective-permute-start = (f32[2,1,16,128]{3,2,1,0:T(8,128)S(1)}, f32[2,1,16,128]{3,2,1,0:T(8,128)S(1)}, u32[]{:S(2)}, u32[]{:S(2)}) collective-permute-start(f32[2,1,16,128]{3,2,1,0:T(8,128)S(1)} %get-tuple-element.31), channel_id=1, source_target_pairs={{1,0},{2,1},{3,2},{5,4},{6,5},{7,6},{9,8},{10,9},{11,10},{13,12},{... | collective-permute-start | bytes 49160 | tf_op jit(solution)/shard_map/ppermute | solution.py:21
  2.1 3.2 %collective-permute-start.1 = (f32[2,1,16,128]{3,2,1,0:T(8,128)S(1)}, f32[2,1,16,128]{3,2,1,0:T(8,128)S(1)}, u32[]{:S(2)}, u32[]{:S(2)}) collective-permute-start(f32[2,1,16,128]{3,2,1,0:T(8,128)S(1)} %get-tuple-element.30), channel_id=1, source_target_pairs={{0,1},{1,2},{2,3},{4,5},{5,6},{6,7},{8,9},{9,10},{10,11},{12,13},{... | collective-permute-start | bytes 49160 | tf_op jit(solution)/shard_map/ppermute | solution.py:19
  5.4 0.4 fusion.136
  6.3 0.5 fusion.143
  7.3 0.4 copy-done.1
  7.7 0.5 fusion.117
  8.2 1.3 %collective-permute-start.2 = (f32[2,1,16,128]{3,2,1,0:T(8,128)S(1)}, f32[2,1,16,128]{3,2,1,0:T(8,128)S(1)}, u32[]{:S(2)}, u32[]{:S(2)}) collective-permute-start(f32[2,1,16,128]{3,2,1,0:T(8,128)S(1)} %get-tuple-element.24), channel_id=1, source_target_pairs={{1,0},{2,1},{3,2},{5,4},{6,5},{7,6},{9,8},{10,9},{11,10},{13,12},{... | collective-permute-start | bytes 49160 | tf_op jit(solution)/shard_map/ppermute | solution.py:21
  9.5 5.1 %collective-permute-start.3 = (f32[2,1,16,128]{3,2,1,0:T(8,128)S(1)}, f32[2,1,16,128]{3,2,1,0:T(8,128)S(1)}, u32[]{:S(2)}, u32[]{:S(2)}) collective-permute-start(f32[2,1,16,128]{3,2,1,0:T(8,128)S(1)} %get-tuple-element.23), channel_id=1, source_target_pairs={{0,1},{1,2},{2,3},{4,5},{5,6},{6,7},{8,9},{9,10},{10,11},{12,13},{... | collective-permute-start | bytes 49160 | tf_op jit(solution)/shard_map/ppermute | solution.py:19
  14.7 0.8 collective-permute-done.3
  15.7 0.5 fusion.101
  16.2 1.3 %collective-permute-start.4 = (f32[2,1,16,128]{3,2,1,0:T(8,128)S(1)}, f32[2,1,16,128]{3,2,1,0:T(8,128)S(1)}, u32[]{:S(2)}, u32[]{:S(2)}) collective-permute-start(f32[2,1,16,128]{3,2,1,0:T(8,128)S(1)} %get-tuple-element.22), channel_id=1, source_target_pairs={{1,0},{2,1},{3,2},{5,4},{6,5},{7,6},{9,8},{10,9},{11,10},{13,12},{... | collective-permute-start | bytes 49160 | tf_op jit(solution)/shard_map/ppermute | solution.py:21
  17.5 4.3 %collective-permute-start.5 = (f32[2,1,16,128]{3,2,1,0:T(8,128)S(1)}, f32[2,1,16,128]{3,2,1,0:T(8,128)S(1)}, u32[]{:S(2)}, u32[]{:S(2)}) collective-permute-start(f32[2,1,16,128]{3,2,1,0:T(8,128)S(1)} %get-tuple-element.21), channel_id=1, source_target_pairs={{0,1},{1,2},{2,3},{4,5},{5,6},{6,7},{8,9},{9,10},{10,11},{12,13},{... | collective-permute-start | bytes 49160 | tf_op jit(solution)/shard_map/ppermute | solution.py:19
  21.9 0.7 collective-permute-done.5
  22.8 0.5 fusion.85
  23.3 1.3 %collective-permute-start.6 = (f32[2,1,16,128]{3,2,1,0:T(8,128)S(1)}, f32[2,1,16,128]{3,2,1,0:T(8,128)S(1)}, u32[]{:S(2)}, u32[]{:S(2)}) collective-permute-start(f32[2,1,16,128]{3,2,1,0:T(8,128)S(1)} %get-tuple-element.20), channel_id=1, source_target_pairs={{1,0},{2,1},{3,2},{5,4},{6,5},{7,6},{9,8},{10,9},{11,10},{13,12},{... | collective-permute-start | bytes 49160 | tf_op jit(solution)/shard_map/ppermute | solution.py:21
  24.6 4.9 %collective-permute-start.7 = (f32[2,1,16,128]{3,2,1,0:T(8,128)S(1)}, f32[2,1,16,128]{3,2,1,0:T(8,128)S(1)}, u32[]{:S(2)}, u32[]{:S(2)}) collective-permute-start(f32[2,1,16,128]{3,2,1,0:T(8,128)S(1)} %get-tuple-element.19), channel_id=1, source_target_pairs={{0,1},{1,2},{2,3},{4,5},{5,6},{6,7},{8,9},{9,10},{10,11},{12,13},{... | collective-permute-start | bytes 49160 | tf_op jit(solution)/shard_map/ppermute | solution.py:19
  29.5 0.8 collective-permute-done.7
  30.5 0.5 fusion.69
  30.9 1.3 %collective-permute-start.8 = (f32[2,1,16,128]{3,2,1,0:T(8,128)S(1)}, f32[2,1,16,128]{3,2,1,0:T(8,128)S(1)}, u32[]{:S(2)}, u32[]{:S(2)}) collective-permute-start(f32[2,1,16,128]{3,2,1,0:T(8,128)S(1)} %get-tuple-element.18), channel_id=1, source_target_pairs={{1,0},{2,1},{3,2},{5,4},{6,5},{7,6},{9,8},{10,9},{11,10},{13,12},{... | collective-permute-start | bytes 49160 | tf_op jit(solution)/shard_map/ppermute | solution.py:21
  32.2 4.9 %collective-permute-start.9 = (f32[2,1,16,128]{3,2,1,0:T(8,128)S(1)}, f32[2,1,16,128]{3,2,1,0:T(8,128)S(1)}, u32[]{:S(2)}, u32[]{:S(2)}) collective-permute-start(f32[2,1,16,128]{3,2,1,0:T(8,128)S(1)} %get-tuple-element.17), channel_id=1, source_target_pairs={{0,1},{1,2},{2,3},{4,5},{5,6},{6,7},{8,9},{9,10},{10,11},{12,13},{... | collective-permute-start | bytes 49160 | tf_op jit(solution)/shard_map/ppermute | solution.py:19
  37.2 0.7 collective-permute-done.9
  38.1 0.5 fusion.53
  38.6 1.3 %collective-permute-start.10 = (f32[2,1,16,128]{3,2,1,0:T(8,128)S(1)}, f32[2,1,16,128]{3,2,1,0:T(8,128)S(1)}, u32[]{:S(2)}, u32[]{:S(2)}) collective-permute-start(f32[2,1,16,128]{3,2,1,0:T(8,128)S(1)} %get-tuple-element.16), channel_id=1, source_target_pairs={{1,0},{2,1},{3,2},{5,4},{6,5},{7,6},{9,8},{10,9},{11,10},{13,12},{... | collective-permute-start | bytes 49160 | tf_op jit(solution)/shard_map/ppermute | solution.py:21
  39.9 4.9 %collective-permute-start.11 = (f32[2,1,16,128]{3,2,1,0:T(8,128)S(1)}, f32[2,1,16,128]{3,2,1,0:T(8,128)S(1)}, u32[]{:S(2)}, u32[]{:S(2)}) collective-permute-start(f32[2,1,16,128]{3,2,1,0:T(8,128)S(1)} %get-tuple-element.15), channel_id=1, source_target_pairs={{0,1},{1,2},{2,3},{4,5},{5,6},{6,7},{8,9},{9,10},{10,11},{12,13},{... | collective-permute-start | bytes 49160 | tf_op jit(solution)/shard_map/ppermute | solution.py:19
  44.8 0.8 collective-permute-done.11
  45.8 0.5 fusion.37
  46.3 1.3 %collective-permute-start.12 = (f32[2,1,16,128]{3,2,1,0:T(8,128)S(1)}, f32[2,1,16,128]{3,2,1,0:T(8,128)S(1)}, u32[]{:S(2)}, u32[]{:S(2)}) collective-permute-start(f32[2,1,16,128]{3,2,1,0:T(8,128)S(1)} %get-tuple-element.14), channel_id=1, source_target_pairs={{1,0},{2,1},{3,2},{5,4},{6,5},{7,6},{9,8},{10,9},{11,10},{13,12},{... | collective-permute-start | bytes 49160 | tf_op jit(solution)/shard_map/ppermute | solution.py:21
  47.6 4.9 %collective-permute-start.13 = (f32[2,1,16,128]{3,2,1,0:T(8,128)S(1)}, f32[2,1,16,128]{3,2,1,0:T(8,128)S(1)}, u32[]{:S(2)}, u32[]{:S(2)}) collective-permute-start(f32[2,1,16,128]{3,2,1,0:T(8,128)S(1)} %get-tuple-element.13), channel_id=1, source_target_pairs={{0,1},{1,2},{2,3},{4,5},{5,6},{6,7},{8,9},{9,10},{10,11},{12,13},{... | collective-permute-start | bytes 49160 | tf_op jit(solution)/shard_map/ppermute | solution.py:19
  52.5 2.9 %cholesky.16 = f32[32,32]{1,0:T(8,128)S(1)} custom-call(f32[32,32]{1,0:T(8,128)S(1)} %fusion.181), custom_call_target="Cholesky" | custom-call | tf_op jit(solution)/shard_map/jit(cholesky)/cholesky | solution.py:158
  55.6 0.5 fusion.21
  56.1 1.3 %collective-permute-start.14 = (f32[2,1,16,128]{3,2,1,0:T(8,128)S(1)}, f32[2,1,16,128]{3,2,1,0:T(8,128)S(1)}, u32[]{:S(2)}, u32[]{:S(2)}) collective-permute-start(f32[2,1,16,128]{3,2,1,0:T(8,128)S(1)} %get-tuple-element.12), channel_id=1, source_target_pairs={{1,0},{2,1},{3,2},{5,4},{6,5},{7,6},{9,8},{10,9},{11,10},{13,12},{... | collective-permute-start | bytes 49160 | tf_op jit(solution)/shard_map/ppermute | solution.py:21
  57.4 4.8 %collective-permute-start.15 = (f32[2,1,16,128]{3,2,1,0:T(8,128)S(1)}, f32[2,1,16,128]{3,2,1,0:T(8,128)S(1)}, u32[]{:S(2)}, u32[]{:S(2)}) collective-permute-start(f32[2,1,16,128]{3,2,1,0:T(8,128)S(1)} %get-tuple-element.11), channel_id=1, source_target_pairs={{0,1},{1,2},{2,3},{4,5},{5,6},{6,7},{8,9},{9,10},{10,11},{12,13},{... | collective-permute-start | bytes 49160 | tf_op jit(solution)/shard_map/ppermute | solution.py:19
  62.3 0.8 collective-permute-done.15
  63.2 0.5 fusion.5
  64.0 0.7 copy.36
  64.6 5.8 %all-to-all-start = ((f32[8,2,128,8]{2,1,3,0:T(2,128)}), f32[8,2,128,8]{2,1,3,0:T(2,128)S(1)}, u32[]{:S(2)}, u32[]{:S(2)}) async-start(f32[8,2,128,8]{2,1,3,0:T(2,128)} %copy.36), calls=%async_computation | async-start | bytes 131072 | tf_op jit(solution)/shard_map/all_to_all | solution.py:144
  70.4 0.7 compare_reduce_fusion
  71.2 6.2 %all-to-all-done = f32[8,2,128,8]{2,1,3,0:T(2,128)S(1)} async-done(((f32[8,2,128,8]{2,1,3,0:T(2,128)}), f32[8,2,128,8]{2,1,3,0:T(2,128)S(1)}, u32[]{:S(2)}, u32[]{:S(2)}) %all-to-all-start) | async-done | bytes 65568 | tf_op jit(solution)/shard_map/all_to_all | solution.py:144
  77.7 0.9 reshape.260
  78.6 5.2 %all-to-all-start.1 = ((f32[4,1,1024]{2,1,0:T(1,128)}), f32[4,1,1024]{2,1,0:T(1,128)S(1)}, u32[]{:S(2)}, u32[]{:S(2)}) async-start(f32[4,1,1024]{2,1,0:T(1,128)} %reshape.260), calls=%async_computation.1 | async-start | bytes 32768 | tf_op jit(solution)/shard_map/all_to_all | solution.py:154
  83.8 0.6 fusion.179
  84.4 2.4 %custom-call.10 = f32[1,32,32]{1,2,0:T(8,128)S(1)} custom-call(f32[1,32,32]{2,1,0:T(8,128)S(1)} %fusion.179), custom_call_target="InvertDiagBlocksLowerTriangular" | custom-call | tf_op jit(solution)/shard_map/jit(_cho_solve)/triangular_solve | solution.py:159
  86.9 0.8 all-to-all-done.1
  87.7 0.5 broadcast.670
  88.2 0.7 reduce.6
  88.9 0.3 reshape.261
  89.6 0.8 fusion.182
  (66 shorter events, 3.8 us)
Async XLA Ops:
  0.0 6.2 %copy-start.4 = (bf16[1,8,16,128]{3,2,1,0:T(8,128)(2,1)S(1)}, bf16[1,8,16,128]{3,2,1,0:T(8,128)(2,1)}, u32[]{:S(2)}) copy-start(bf16[1,8,16,128]{3,2,1,0:T(8,128)(2,1)} %param.15) | copy-start | bytes 98308
  0.0 6.2 %copy-start.5 = (bf16[1,8,16,128]{3,2,1,0:T(8,128)(2,1)S(1)}, bf16[1,8,16,128]{3,2,1,0:T(8,128)(2,1)}, u32[]{:S(2)}) copy-start(bf16[1,8,16,128]{3,2,1,0:T(8,128)(2,1)} %param.14) | copy-start | bytes 98308
  0.7 6.1 %collective-permute-start = (f32[2,1,16,128]{3,2,1,0:T(8,128)S(1)}, f32[2,1,16,128]{3,2,1,0:T(8,128)S(1)}, u32[]{:S(2)}, u32[]{:S(2)}) collective-permute-start(f32[2,1,16,128]{3,2,1,0:T(8,128)S(1)} %get-tuple-element.31), channel_id=1, source_target_pairs={{1,0},{2,1},{3,2},{5,4},{6,5},{7,6},{9,8},{10,9},{11,10},{13,12},{... | collective-permute-start | bytes 49160 | tf_op jit(solution)/shard_map/ppermute | solution.py:21
  2.0 3.3 %copy-start.6 = (s32[8]{0:T(128)S(1)}, s32[8]{0:T(128)}, u32[]{:S(2)}) copy-start(s32[8]{0:T(128)} %param.16) | copy-start | bytes 100
  2.0 3.3 %copy-start.8 = (s32[32]{0:T(128)S(1)}, s32[32]{0:T(128)}, u32[]{:S(2)}) copy-start(s32[32]{0:T(128)} %param.17) | copy-start | bytes 388
  2.1 3.9 %copy-start.7 = (s32[32]{0:T(128)S(1)}, s32[32]{0:T(128)}, u32[]{:S(2)}) copy-start(s32[32]{0:T(128)} %param.18) | copy-start | bytes 388
  2.1 4.0 %copy-start.9 = (f32[32]{0:T(128)S(1)}, f32[32]{0:T(128)}, u32[]{:S(2)}) copy-start(f32[32]{0:T(128)} %param.19) | copy-start | bytes 388
  2.1 4.1 %copy-start.2 = (bf16[1,8,16,128]{3,2,1,0:T(8,128)(2,1)S(1)}, bf16[1,8,16,128]{3,2,1,0:T(8,128)(2,1)}, u32[]{:S(2)}) copy-start(bf16[1,8,16,128]{3,2,1,0:T(8,128)(2,1)} %param.13) | copy-start | bytes 98308
  2.1 4.1 %copy-start.3 = (bf16[1,8,16,128]{3,2,1,0:T(8,128)(2,1)S(1)}, bf16[1,8,16,128]{3,2,1,0:T(8,128)(2,1)}, u32[]{:S(2)}) copy-start(bf16[1,8,16,128]{3,2,1,0:T(8,128)(2,1)} %param.12) | copy-start | bytes 98308
  2.1 4.7 %collective-permute-start.1 = (f32[2,1,16,128]{3,2,1,0:T(8,128)S(1)}, f32[2,1,16,128]{3,2,1,0:T(8,128)S(1)}, u32[]{:S(2)}, u32[]{:S(2)}) collective-permute-start(f32[2,1,16,128]{3,2,1,0:T(8,128)S(1)} %get-tuple-element.30), channel_id=1, source_target_pairs={{0,1},{1,2},{2,3},{4,5},{5,6},{6,7},{8,9},{9,10},{10,11},{12,13},{... | collective-permute-start | bytes 49160 | tf_op jit(solution)/shard_map/ppermute | solution.py:19
  6.2 0.9 %copy-start = (f32[1,2,8,16,128]{4,3,2,1,0:T(8,128)S(1)}, f32[1,2,8,16,128]{4,3,2,1,0:T(8,128)}, u32[]{:S(2)}) copy-start(f32[1,2,8,16,128]{4,3,2,1,0:T(8,128)} %param.11) | copy-start | bytes 393220
  6.8 0.9 %copy-start.1 = (f32[1,2,8,16,128]{4,3,2,1,0:T(8,128)S(1)}, f32[1,2,8,16,128]{4,3,2,1,0:T(8,128)}, u32[]{:S(2)}) copy-start(f32[1,2,8,16,128]{4,3,2,1,0:T(8,128)} %param.10) | copy-start | bytes 393220
  8.2 6.4 %collective-permute-start.2 = (f32[2,1,16,128]{3,2,1,0:T(8,128)S(1)}, f32[2,1,16,128]{3,2,1,0:T(8,128)S(1)}, u32[]{:S(2)}, u32[]{:S(2)}) collective-permute-start(f32[2,1,16,128]{3,2,1,0:T(8,128)S(1)} %get-tuple-element.24), channel_id=1, source_target_pairs={{1,0},{2,1},{3,2},{5,4},{6,5},{7,6},{9,8},{10,9},{11,10},{13,12},{... | collective-permute-start | bytes 49160 | tf_op jit(solution)/shard_map/ppermute | solution.py:21
  9.5 6.0 %collective-permute-start.3 = (f32[2,1,16,128]{3,2,1,0:T(8,128)S(1)}, f32[2,1,16,128]{3,2,1,0:T(8,128)S(1)}, u32[]{:S(2)}, u32[]{:S(2)}) collective-permute-start(f32[2,1,16,128]{3,2,1,0:T(8,128)S(1)} %get-tuple-element.23), channel_id=1, source_target_pairs={{0,1},{1,2},{2,3},{4,5},{5,6},{6,7},{8,9},{9,10},{10,11},{12,13},{... | collective-permute-start | bytes 49160 | tf_op jit(solution)/shard_map/ppermute | solution.py:19
  16.2 5.7 %collective-permute-start.4 = (f32[2,1,16,128]{3,2,1,0:T(8,128)S(1)}, f32[2,1,16,128]{3,2,1,0:T(8,128)S(1)}, u32[]{:S(2)}, u32[]{:S(2)}) collective-permute-start(f32[2,1,16,128]{3,2,1,0:T(8,128)S(1)} %get-tuple-element.22), channel_id=1, source_target_pairs={{1,0},{2,1},{3,2},{5,4},{6,5},{7,6},{9,8},{10,9},{11,10},{13,12},{... | collective-permute-start | bytes 49160 | tf_op jit(solution)/shard_map/ppermute | solution.py:21
  17.5 5.1 %collective-permute-start.5 = (f32[2,1,16,128]{3,2,1,0:T(8,128)S(1)}, f32[2,1,16,128]{3,2,1,0:T(8,128)S(1)}, u32[]{:S(2)}, u32[]{:S(2)}) collective-permute-start(f32[2,1,16,128]{3,2,1,0:T(8,128)S(1)} %get-tuple-element.21), channel_id=1, source_target_pairs={{0,1},{1,2},{2,3},{4,5},{5,6},{6,7},{8,9},{9,10},{10,11},{12,13},{... | collective-permute-start | bytes 49160 | tf_op jit(solution)/shard_map/ppermute | solution.py:19
  23.3 6.2 %collective-permute-start.6 = (f32[2,1,16,128]{3,2,1,0:T(8,128)S(1)}, f32[2,1,16,128]{3,2,1,0:T(8,128)S(1)}, u32[]{:S(2)}, u32[]{:S(2)}) collective-permute-start(f32[2,1,16,128]{3,2,1,0:T(8,128)S(1)} %get-tuple-element.20), channel_id=1, source_target_pairs={{1,0},{2,1},{3,2},{5,4},{6,5},{7,6},{9,8},{10,9},{11,10},{13,12},{... | collective-permute-start | bytes 49160 | tf_op jit(solution)/shard_map/ppermute | solution.py:21
  24.6 5.7 %collective-permute-start.7 = (f32[2,1,16,128]{3,2,1,0:T(8,128)S(1)}, f32[2,1,16,128]{3,2,1,0:T(8,128)S(1)}, u32[]{:S(2)}, u32[]{:S(2)}) collective-permute-start(f32[2,1,16,128]{3,2,1,0:T(8,128)S(1)} %get-tuple-element.19), channel_id=1, source_target_pairs={{0,1},{1,2},{2,3},{4,5},{5,6},{6,7},{8,9},{9,10},{10,11},{12,13},{... | collective-permute-start | bytes 49160 | tf_op jit(solution)/shard_map/ppermute | solution.py:19
  30.9 6.3 %collective-permute-start.8 = (f32[2,1,16,128]{3,2,1,0:T(8,128)S(1)}, f32[2,1,16,128]{3,2,1,0:T(8,128)S(1)}, u32[]{:S(2)}, u32[]{:S(2)}) collective-permute-start(f32[2,1,16,128]{3,2,1,0:T(8,128)S(1)} %get-tuple-element.18), channel_id=1, source_target_pairs={{1,0},{2,1},{3,2},{5,4},{6,5},{7,6},{9,8},{10,9},{11,10},{13,12},{... | collective-permute-start | bytes 49160 | tf_op jit(solution)/shard_map/ppermute | solution.py:21
  32.2 5.7 %collective-permute-start.9 = (f32[2,1,16,128]{3,2,1,0:T(8,128)S(1)}, f32[2,1,16,128]{3,2,1,0:T(8,128)S(1)}, u32[]{:S(2)}, u32[]{:S(2)}) collective-permute-start(f32[2,1,16,128]{3,2,1,0:T(8,128)S(1)} %get-tuple-element.17), channel_id=1, source_target_pairs={{0,1},{1,2},{2,3},{4,5},{5,6},{6,7},{8,9},{9,10},{10,11},{12,13},{... | collective-permute-start | bytes 49160 | tf_op jit(solution)/shard_map/ppermute | solution.py:19
  38.6 6.2 %collective-permute-start.10 = (f32[2,1,16,128]{3,2,1,0:T(8,128)S(1)}, f32[2,1,16,128]{3,2,1,0:T(8,128)S(1)}, u32[]{:S(2)}, u32[]{:S(2)}) collective-permute-start(f32[2,1,16,128]{3,2,1,0:T(8,128)S(1)} %get-tuple-element.16), channel_id=1, source_target_pairs={{1,0},{2,1},{3,2},{5,4},{6,5},{7,6},{9,8},{10,9},{11,10},{13,12},{... | collective-permute-start | bytes 49160 | tf_op jit(solution)/shard_map/ppermute | solution.py:21
  39.9 5.7 %collective-permute-start.11 = (f32[2,1,16,128]{3,2,1,0:T(8,128)S(1)}, f32[2,1,16,128]{3,2,1,0:T(8,128)S(1)}, u32[]{:S(2)}, u32[]{:S(2)}) collective-permute-start(f32[2,1,16,128]{3,2,1,0:T(8,128)S(1)} %get-tuple-element.15), channel_id=1, source_target_pairs={{0,1},{1,2},{2,3},{4,5},{5,6},{6,7},{8,9},{9,10},{10,11},{12,13},{... | collective-permute-start | bytes 49160 | tf_op jit(solution)/shard_map/ppermute | solution.py:19
  46.3 9.1 %collective-permute-start.12 = (f32[2,1,16,128]{3,2,1,0:T(8,128)S(1)}, f32[2,1,16,128]{3,2,1,0:T(8,128)S(1)}, u32[]{:S(2)}, u32[]{:S(2)}) collective-permute-start(f32[2,1,16,128]{3,2,1,0:T(8,128)S(1)} %get-tuple-element.14), channel_id=1, source_target_pairs={{1,0},{2,1},{3,2},{5,4},{6,5},{7,6},{9,8},{10,9},{11,10},{13,12},{... | collective-permute-start | bytes 49160 | tf_op jit(solution)/shard_map/ppermute | solution.py:21
  47.6 7.8 %collective-permute-start.13 = (f32[2,1,16,128]{3,2,1,0:T(8,128)S(1)}, f32[2,1,16,128]{3,2,1,0:T(8,128)S(1)}, u32[]{:S(2)}, u32[]{:S(2)}) collective-permute-start(f32[2,1,16,128]{3,2,1,0:T(8,128)S(1)} %get-tuple-element.13), channel_id=1, source_target_pairs={{0,1},{1,2},{2,3},{4,5},{5,6},{6,7},{8,9},{9,10},{10,11},{12,13},{... | collective-permute-start | bytes 49160 | tf_op jit(solution)/shard_map/ppermute | solution.py:19
  56.1 6.2 %collective-permute-start.14 = (f32[2,1,16,128]{3,2,1,0:T(8,128)S(1)}, f32[2,1,16,128]{3,2,1,0:T(8,128)S(1)}, u32[]{:S(2)}, u32[]{:S(2)}) collective-permute-start(f32[2,1,16,128]{3,2,1,0:T(8,128)S(1)} %get-tuple-element.12), channel_id=1, source_target_pairs={{1,0},{2,1},{3,2},{5,4},{6,5},{7,6},{9,8},{10,9},{11,10},{13,12},{... | collective-permute-start | bytes 49160 | tf_op jit(solution)/shard_map/ppermute | solution.py:21
  57.4 5.7 %collective-permute-start.15 = (f32[2,1,16,128]{3,2,1,0:T(8,128)S(1)}, f32[2,1,16,128]{3,2,1,0:T(8,128)S(1)}, u32[]{:S(2)}, u32[]{:S(2)}) collective-permute-start(f32[2,1,16,128]{3,2,1,0:T(8,128)S(1)} %get-tuple-element.11), channel_id=1, source_target_pairs={{0,1},{1,2},{2,3},{4,5},{5,6},{6,7},{8,9},{9,10},{10,11},{12,13},{... | collective-permute-start | bytes 49160 | tf_op jit(solution)/shard_map/ppermute | solution.py:19
  64.6 12.7 %all-to-all-start = ((f32[8,2,128,8]{2,1,3,0:T(2,128)}), f32[8,2,128,8]{2,1,3,0:T(2,128)S(1)}, u32[]{:S(2)}, u32[]{:S(2)}) async-start(f32[8,2,128,8]{2,1,3,0:T(2,128)} %copy.36), calls=%async_computation | async-start | bytes 131072 | tf_op jit(solution)/shard_map/all_to_all | solution.py:144
  78.6 9.1 %all-to-all-start.1 = ((f32[4,1,1024]{2,1,0:T(1,128)}), f32[4,1,1024]{2,1,0:T(1,128)S(1)}, u32[]{:S(2)}, u32[]{:S(2)}) async-start(f32[4,1,1024]{2,1,0:T(1,128)} %reshape.260), calls=%async_computation.1 | async-start | bytes 32768 | tf_op jit(solution)/shard_map/all_to_all | solution.py:154
where the time goes:
time: 91.3 us; the launch traced here: 90.5 us
  starting transfers between devices  58.2 us (64%)
  other arithmetic  14.4 us (16%)
  waiting for transfers between devices  11.6 us (13%)
  local copies, waits for them, and re-layouts  4.18 us (5%)
  matrix products  1.58 us (2%)
    ppermute x8, starting transfers between devices, with_halo(): lax.ppermute(tail, axis, [(i, (i + 1) % count) for i in range(ends)])  36.8 us
    ppermute x8, starting transfers between devices, with_halo(): lax.ppermute(head, axis, [((i + 1) % count, i) for i in range(ends)])  10.3 us
    all_to_all x1, waiting for transfers between devices, shards(): lax.all_to_all(parcels, 'shot', split_axis=0, concat_axis=0, tiled=True)  6.15 us
    all_to_all x1, starting transfers between devices, shards(): lax.all_to_all(parcels, 'shot', split_axis=0, concat_axis=0, tiled=True)  5.81 us
    all_to_all x1, starting transfers between devices, shards(): lax.all_to_all(owned, 'depth', split_axis=1, concat_axis=2, tiled=True)  5.21 us
    ppermute x8, waiting for transfers between devices, with_halo(): lax.ppermute(tail, axis, [(i, (i + 1) % count) for i in range(ends)])  4.61 us
    add x8, other arithmetic, shards(): 2.0 * current - earlier_field + apply_operator(extended, weights)  3.72 us
    another operation x3, other arithmetic, shards(): factor = jnp.linalg.cholesky(matrix)  3.6 us
  transfers between devices with their start and end apart: 18, of which 8 were waited for; matrix products, arithmetic and copies ran while one was open for 9% of the time, Pallas kernels for 0%

commit v1 on v0

v1 whole, which is shorter than its diff:
```python
import functools

import jax
import jax.numpy as jnp
from jax import lax
from jax.experimental import pallas as pl
from jax.experimental.pallas import tpu as pltpu
from jax.sharding import PartitionSpec as P

NT = 8
IMB = 4
WMAX = 4
PAD = 8
MESH = pl.DeviceIdType.MESH
SINE = (
    1.0,
    -1.0 / 6,
    1.0 / 120,
    -1.0 / 5040,
    1.0 / 362880,
    -1.0 / 39916800,
    1.0 / 6227020800,
)
COSINE = (
    1.0,
    -1.0 / 2,
    1.0 / 24,
    -1.0 / 720,
    1.0 / 40320,
    -1.0 / 3628800,
    1.0 / 479001600,
)


def series(square, terms):
    total = jnp.full_like(square, terms[-1])
    for term in terms[-2::-1]:
        total = total * square + term
    return total


def sine_cosine(angle):
    square = angle * angle
    return angle * series(square, SINE), series(square, COSINE)


def store_weights(raw, weights, layers):
    speed, ratio, theta, sweep = (raw[i, layers].astype(jnp.float32) for i in range(4))
    sine, axis_z = sine_cosine(theta)
    half_sine, half_cosine = sine_cosine(0.5 * sweep)
    axis_x = sine * (1.0 - 2.0 * half_sine * half_sine)
    axis_y = sine * (2.0 * half_sine * half_cosine)
    pull = speed * ratio
    base = speed + 2.0 * pull
    skew = -2.0 * pull
    skew_z, skew_x = skew * axis_z, skew * axis_x
    along_z = base + skew_z * axis_z
    along_x = base + skew_x * axis_x
    along_y = base + skew * axis_y * axis_y
    weights[0, layers] = 2.0 - 2.0 * (along_z + along_x + along_y)
    weights[1, layers] = along_z
    weights[2, layers] = along_x
    weights[3, layers] = along_y
    weights[4, layers] = 0.5 * (skew_z * axis_x)
    weights[5, layers] = 0.5 * (skew_z * axis_y)
    weights[6, layers] = 0.5 * (skew_x * axis_y)


def negative_inverse(matrix):
    size = matrix.shape[0]
    row_ids = lax.broadcasted_iota(jnp.int32, (size, size), 0)
    column_ids = lax.broadcasted_iota(jnp.int32, (size, size), 1)
    active = list(range(size // WMAX))
    while active:
        chosen, active = active[0::2], active[1::2]
        for inner in range(WMAX):
            pivots = [WMAX * block + inner for block in chosen]
            parts = []
            for k in pivots:
                row = matrix[k : k + 1, :]
                column = matrix[:, k : k + 1]
                inverse = 1.0 / matrix[k : k + 1, k : k + 1]
                parts.append((k, row * inverse, column, column * inverse, inverse))
            for k, row, column, scaled, inverse in parts:
                matrix = matrix - column * row
            for k, row, column, scaled, inverse in parts:
                matrix = jnp.where(row_ids == k, jnp.broadcast_to(row, matrix.shape), matrix)
            for k, row, column, scaled, inverse in parts:
                edge = jnp.where(row_ids[:, :1] == k, -inverse, scaled)
                matrix = jnp.where(column_ids == k, jnp.broadcast_to(edge, matrix.shape), matrix)
    return matrix


def band_matrix(widths, damp):
    size = widths.shape[1]
    row_ids = lax.broadcasted_iota(jnp.int32, (size, size), 0)
    column_ids = lax.broadcasted_iota(jnp.int32, (size, size), 1)
    same = row_ids == column_ids
    across = jnp.broadcast_to(widths.astype(jnp.float32), (size, size))
    down = jnp.sum(jnp.where(same, across, 0.0), axis=1, keepdims=True)
    distance = jnp.abs(row_ids - column_ids)
    reach = jnp.maximum(across, jnp.broadcast_to(down, (size, size)))
    near = jnp.where(distance.astype(jnp.float32) <= reach, 1.0, 0.0)
    adjacent = jnp.where(same, 0.0, near)
    diagonal = damp + jnp.sum(adjacent, axis=0, keepdims=True)
    return jnp.where(same, jnp.broadcast_to(diagonal, (size, size)), -adjacent)


def kernel(
    shots,
    depths,
    anchor,
    slots,
    widths,
    damp,
    prev_fields,
    cur_fields,
    speed_term,
    epsilon,
    tilt,
    azimuth,
    out,
    even,
    odd,
    raw,
    weights,
    picture,
    rows,
    parcels,
    arrived,
    packed,
    traces,
    inverse,
    local_sem,
    halo_send,
    halo_recv,
    shot_send,
    shot_recv,
    depth_send,
    depth_recv,
):
    shot = lax.axis_index("shot")
    depth = lax.axis_index("depth")
    slab = speed_term.shape[1]
    span = speed_term.shape[2]
    lanes = speed_term.shape[3]
    blocks = slots.shape[0]
    half = slab // 2
    top = 3 * slab
    inner = pl.ds(PAD, span)

    barrier = pltpu.get_barrier_semaphore()
    for o in range(1, depths):
        peer = {"depth": lax.rem(depth + o, depths)}
        pl.semaphore_signal(barrier, inc=1, device_id=peer, device_id_type=MESH)
    for o in range(1, shots):
        peer = {"shot": lax.rem(shot + o, shots)}
        pl.semaphore_signal(barrier, inc=1, device_id=peer, device_id_type=MESH)

    params = (speed_term, epsilon, tilt, azimuth)

    def source(i, first, last):
        if i < 2:
            return (cur_fields, prev_fields)[i].at[0, :, pl.ds(first, last - first)]
        return params[i - 2].at[0, pl.ds(first, last - first)]

    def target(i, first, last):
        if i < 2:
            return (even, odd)[i].at[:, pl.ds(first, last - first), inner]
        return raw.at[i - 2, pl.ds(first, last - first)]

    local = [
        pltpu.make_async_copy(source(i, 0, slab), target(i, slab, 2 * slab), local_sem.at[i])
        for i in range(6)
    ]
    for copy in local:
        copy.start()
    pl.semaphore_wait(barrier, depths + shots - 2)

    def halo(side, chunk, i):
        cut = 0 if i == 0 else 1
        if side == 0:
            first, last = ((half, slab), (cut, half))[chunk]
            place = first
            step = 1
        else:
            first, last = ((0, half), (half, slab - cut))[chunk]
            place = 2 * slab + first
            step = -1
        return pltpu.make_async_remote_copy(
            src_ref=source(i, first, last),
            dst_ref=target(i, place, place + last - first),
            send_sem=halo_send.at[side, chunk, i],
            recv_sem=halo_recv.at[side, chunk, i],
            device_id={"depth": lax.rem(depth + step + depths, depths)},
            device_id_type=MESH,
        )

    has_next = depth < depths - 1
    has_before = depth > 0
    for chunk in range(2):

        @pl.when(has_next)
        def _():
            for i in range(6):
                halo(0, chunk, i).start()

        @pl.when(has_before)
        def _():
            for i in range(6):
                halo(1, chunk, i).start()

    margin = jnp.zeros((2, top, PAD, lanes), jnp.float32)
    for field in (even, odd):
        field[:, :, 0:PAD] = margin
        field[:, :, PAD + span : 2 * PAD + span] = margin

    def clear(first):
        layers = pl.ds(first, slab)
        for field in (even, odd):
            field[:, layers, inner] = jnp.zeros((2, slab, span, lanes), jnp.float32)
        for i in range(4):
            raw[i, layers] = jnp.zeros((slab, span, lanes), raw.dtype)

    pl.when(jnp.logical_not(has_before))(lambda: clear(0))
    pl.when(jnp.logical_not(has_next))(lambda: clear(2 * slab))

    for copy in local:
        copy.wait()
    for first in range(slab, 2 * slab, 2):
        store_weights(raw, weights, pl.ds(first, 2))
    inverse[...] = negative_inverse(band_matrix(widths[...], damp[...]))
    picture[...] = jnp.zeros(picture.shape, jnp.float32)

    lane_ids = lax.broadcasted_iota(jnp.int32, (2, span, lanes), 2)
    not_first = lane_ids > 0
    not_last = lane_ids < lanes - 1

    def beside(value):
        after = jnp.where(not_last, pltpu.roll(value, lanes - 1, 2), 0.0)
        before = jnp.where(not_first, pltpu.roll(value, 1, 2), 0.0)
        return after, before

    def layer_parts(now, z, whole):
        center = now[:, z, PAD : PAD + span]
        after_x = now[:, z, PAD + 1 : PAD + 1 + span]
        before_x = now[:, z, PAD - 1 : PAD - 1 + span]
        after_y, before_y = beside(center)
        slope_x = after_x - before_x
        slope_y = after_y - before_y
        if not whole:
            return center, slope_x, slope_y
        after_xy, before_xy = beside(slope_x)
        return (
            center,
            slope_x,
            slope_y,
            after_x + before_x,
            after_y + before_y,
            after_xy - before_xy,
        )

    def advance(now, new, first, last, own):
        below = layer_parts(now, first - 1, False)
        here = layer_parts(now, first, True)
        for z in range(first, last):
            above = layer_parts(now, z + 1, z + 1 < last)
            center, _, _, sum_x, sum_y, cross_xy = here
            w = [weights[i, z][None] for i in range(7)]
            total = w[0] * center - new[:, z, PAD : PAD + span]
            total = total + w[1] * (above[0] + below[0])
            total = total + w[2] * sum_x
            total = total + w[3] * sum_y
            total = total + w[4] * (above[1] - below[1])
            total = total + w[5] * (above[2] - below[2])
            total = total + w[6] * cross_xy
            new[:, z, PAD : PAD + span] = total
            if own and slab <= z < 2 * slab:
                picture[z - slab] += total[0] * total[1]
            below, here = here, above

    def arrive(chunk):
        @pl.when(has_before)
        def _():
            for i in range(6):
                halo(0, chunk, i).wait_recv()

        @pl.when(has_next)
        def _():
            for i in range(6):
                halo(1, chunk, i).wait_recv()

    fields = (even, odd)
    arrive(0)
    for first in range(half, slab, 2):
        store_weights(raw, weights, pl.ds(first, 2))
        store_weights(raw, weights, pl.ds(2 * slab + first - half, 2))
    for t in range(1, half + 1):
        now, new = fields[(t - 1) % 2], fields[t % 2]
        advance(now, new, half + t, top - half - t, True)
    arrive(1)
    for first, count in ((1, half - 1), (top - half, half - 1)):
        store_weights(raw, weights, pl.ds(first, count))
    for t in range(1, half + 1):
        now, new = fields[(t - 1) % 2], fields[t % 2]
        advance(now, new, t, half + t, False)
        advance(now, new, top - half - t, top - t, False)
    for t in range(half + 1, NT + 1):
        now, new = fields[(t - 1) % 2], fields[t % 2]
        advance(now, new, t, top - t, True)

    rows[...] = jnp.swapaxes(picture[...], 0, 1)

    my_anchor = anchor[shot]

    def parcel(o):
        return pltpu.make_async_remote_copy(
            src_ref=parcels.at[o],
            dst_ref=arrived.at[o],
            send_sem=shot_send.at[o],
            recv_sem=shot_recv.at[o],
            device_id={"shot": lax.rem(shot + o, shots)},
            device_id_type=MESH,
        )

    for o in list(range(1, shots)) + [0]:
        holder = lax.rem(shot + o, shots)
        lowest = slots[holder * IMB]
        for j in range(1, IMB):
            lowest = jnp.minimum(lowest, slots[holder * IMB + j])
        for c in range(2):
            near = lowest + c - my_anchor
            far = near + blocks // 2
            near_in = (near >= 0) & (near < span)
            far_in = (far >= 0) & (far < span)
            index = jnp.where(near_in, near, jnp.where(far_in, far, 0))
            gain = jnp.where(near_in | far_in, 1.0 / NT, 0.0).astype(jnp.float32)
            value = rows[index] * gain
            if o == 0:
                arrived[0, c] = value
            else:
                parcels[o, c] = value
        if o > 0:
            parcel(o).start()

    owned = [jnp.zeros((slab, lanes), jnp.float32) for _ in range(IMB)]
    held = [slots[shot * IMB + j] for j in range(IMB)]
    for o in range(shots):
        if o > 0:
            parcel(o).wait_recv()
        pair = arrived[o]
        from_anchor = anchor[lax.rem(shot + shots - o, shots)]
        for j in range(IMB):
            place = held[j] - from_anchor
            inside = (place >= 0) & (place < span)
            value = jnp.where(lax.rem(held[j], 2) == 0, pair[0], pair[1])
            owned[j] = owned[j] + jnp.where(inside, value, 0.0)

    share = lanes // depths
    lane_row = lax.broadcasted_iota(jnp.int32, (slab, lanes), 1)

    def slice_for(o):
        return pltpu.make_async_remote_copy(
            src_ref=packed.at[o],
            dst_ref=traces.at[pl.ds(pl.multiple_of(depth * slab, slab), slab)],
            send_sem=depth_send.at[o],
            recv_sem=depth_recv.at[o],
            device_id={"depth": lax.rem(depth + o, depths)},
            device_id_type=MESH,
        )

    for o in list(range(1, depths)) + [0]:
        peer = lax.rem(depth + o, depths)
        block = jnp.zeros((slab, lanes), jnp.float32)
        for j in range(IMB):
            shift = lax.rem(j * share - peer * share + lanes, lanes)
            moved = pltpu.roll(owned[j], shift, 1)
            here = (lane_row >= j * share) & (lane_row < (j + 1) * share)
            block = jnp.where(here, moved, block)
        if o == 0:
            traces[pl.ds(pl.multiple_of(depth * slab, slab), slab)] = block
        else:
            packed[o] = block
            slice_for(o).start()
    for o in range(1, depths):
        slice_for(o).wait_recv()
    solved = lax.dot_general(
        traces[...],
        inverse[...],
        (((0,), (0,)), ((), ())),
        precision=lax.Precision.HIGHEST,
        preferred_element_type=jnp.float32,
    )
    out[...] = -solved[: IMB * share].reshape(out.shape)

    for chunk in range(2):

        @pl.when(has_next)
        def _():
            for i in range(6):
                halo(0, chunk, i).wait_send()

        @pl.when(has_before)
        def _():
            for i in range(6):
                halo(1, chunk, i).wait_send()

    for o in range(1, shots):
        parcel(o).wait_send()
    for o in range(1, depths):
        slice_for(o).wait_send()


def shards(
    shots,
    depths,
    prev_fields,
    cur_fields,
    speed_term,
    epsilon,
    tilt,
    azimuth,
    aperture_anchor,
    slot_block,
    band_width,
    depth_damp,
):
    slab, span, lanes = speed_term.shape[1:]
    total = band_width.shape[0]
    f32 = jnp.float32
    smem = pl.BlockSpec(memory_space=pltpu.SMEM)
    vmem = pl.BlockSpec(memory_space=pltpu.VMEM)
    anywhere = pl.BlockSpec(memory_space=pl.ANY)
    return pl.pallas_call(
        functools.partial(kernel, shots, depths),
        name="migrate",
        out_shape=jax.ShapeDtypeStruct((IMB, lanes // depths, total), f32),
        in_specs=[smem, smem, vmem, vmem] + [anywhere] * 6,
        out_specs=vmem,
        scratch_shapes=[
            pltpu.VMEM((2, 3 * slab, span + 2 * PAD, lanes), f32),
            pltpu.VMEM((2, 3 * slab, span + 2 * PAD, lanes), f32),
            pltpu.VMEM((4, 3 * slab, span, lanes), speed_term.dtype),
            pltpu.VMEM((7, 3 * slab, span, lanes), f32),
            pltpu.VMEM((slab, span, lanes), f32),
            pltpu.VMEM((span, slab, lanes), f32),
            pltpu.VMEM((shots, 2, slab, lanes), f32),
            pltpu.VMEM((shots, 2, slab, lanes), f32),
            pltpu.VMEM((depths, slab, lanes), f32),
            pltpu.VMEM((total, lanes), f32),
            pltpu.VMEM((total, total), f32),
            pltpu.SemaphoreType.DMA((6,)),
            pltpu.SemaphoreType.DMA((2, 2, 6)),
            pltpu.SemaphoreType.DMA((2, 2, 6)),
            pltpu.SemaphoreType.DMA((shots,)),
            pltpu.SemaphoreType.DMA((shots,)),
            pltpu.SemaphoreType.DMA((depths,)),
            pltpu.SemaphoreType.DMA((depths,)),
        ],
        compiler_params=pltpu.CompilerParams(
            collective_id=0, has_side_effects=True, vmem_limit_bytes=48 * 1024 * 1024
        ),
    )(
        aperture_anchor,
        slot_block,
        band_width.reshape(1, total),
        depth_damp.reshape(1, total),
        prev_fields,
        cur_fields,
        speed_term,
        epsilon,
        tilt,
        azimuth,
    )


def solution(mesh):
    placed = (
        P("shot", None, "depth", None, None),
        P("shot", None, "depth", None, None),
        P("shot", "depth", None, None),
        P("shot", "depth", None, None),
        P("shot", "depth", None, None),
        P("shot", "depth", None, None),
        P(),
        P(),
        P(),
        P(),
    )
    return jax.shard_map(
        functools.partial(shards, mesh.shape["shot"], mesh.shape["depth"]),
        mesh=mesh,
        in_specs=placed,
        out_specs=P("shot", "depth", None),
        check_vma=False,
    )
```

time: 91.3 us -> 27.6 us (0.30)
  starting transfers between devices: 58.2 us -> 0 us
  Pallas kernels: 0 us -> 21 us
  other arithmetic: 14.4 us -> 0 us
  waiting for transfers between devices: 11.6 us -> 0 us
  local copies, waits for them, and re-layouts: 4.18 us -> 6.17 us
  matrix products: 1.58 us -> 0 us
    ppermute x16 -> x0, starting transfers between devices: 47.2 us -> none  [the longest x8 36.8 us: with_halo(): lax.ppermute(tail, axis, [(i, (i + 1) % count) for i in range(ends)])]
    pallas_call x0 -> x1, Pallas kernels: none -> 21 us  [shards(): pl.pallas_call(functools.partial(kernel, shots, depths), name='migrate',...]
    all_to_all x2 -> x0, starting transfers between devices: 11 us -> none  [the longest x1 5.81 us: shards(): lax.all_to_all(parcels, 'shot', split_axis=0, concat_axis=0, tiled=True)]
    all_to_all x2 -> x0, waiting for transfers between devices: 6.93 us -> none  [the longest x1 6.15 us: shards(): lax.all_to_all(parcels, 'shot', split_axis=0, concat_axis=0, tiled=True)]
    another operation x5 -> x0, other arithmetic: 6.67 us -> none  [the longest x3 3.6 us: shards(): factor = jnp.linalg.cholesky(matrix)]
    ppermute x16 -> x0, waiting for transfers between devices: 4.64 us -> none  [the longest x8 4.61 us: with_halo(): lax.ppermute(tail, axis, [(i, (i + 1) % count) for i in range(ends)])]
    unnamed x22 -> x21, local copies, waits for them, and re-layouts: 1.95 us -> 6.17 us
    add x10 -> x0, other arithmetic: 3.79 us -> none  [the longest x8 3.72 us: shards(): 2.0 * current - earlier_field + apply_operator(extended, weights)]
  transfers between devices with their start and end apart: 18 -> 0, of which waited for: 8 -> 0; matrix products, arithmetic and copies ran while one was open for 9% -> 0% of each run, Pallas kernels for 0% -> 0%
where the time goes in v1:
time: 27.6 us; the launch traced here: 27.2 us
  Pallas kernels  21 us (76%)
  local copies, waits for them, and re-layouts  6.17 us (22%)
    pallas_call x1, Pallas kernels, shards(): pl.pallas_call(functools.partial(kernel, shots, depths), name='migrate',...  21 us
    unnamed x21, local copies, waits for them, and re-layouts  6.17 us

profile of v1, /device:TPU:0, one launch (start us, length us, event | category | flops | bytes accessed | tf_op | source)
XLA Modules:
  0.0 27.2 jit_solution(11016589831221772149)
XLA Ops:
  0.0 0.0 copy-start.9
  0.0 0.0 copy-start.6
  0.0 0.0 copy-start.7
  0.0 0.0 copy-start.8
  0.0 0.6 %copy-done.9 = f32[32]{0:T(128)S(1)} copy-done((f32[32]{0:T(128)S(1)}, f32[32]{0:T(128)}, u32[]{:S(2)}) %copy-start.9) | copy-done | bytes 152
  0.7 0.0 copy-done.6
  0.7 0.0 copy-done.7
  0.7 0.0 copy-done.8
  0.7 0.0 copy-start
  0.7 0.9 %copy-done = f32[1,2,8,16,128]{4,3,2,1,0:T(8,128)S(1)} copy-done((f32[1,2,8,16,128]{4,3,2,1,0:T(8,128)S(1)}, f32[1,2,8,16,128]{4,3,2,1,0:T(8,128)}, u32[]{:S(2)}) %copy-start) | copy-done | bytes 131096
  1.6 0.0 copy-start.1
  1.6 0.9 %copy-done.1 = f32[1,2,8,16,128]{4,3,2,1,0:T(8,128)S(1)} copy-done((f32[1,2,8,16,128]{4,3,2,1,0:T(8,128)S(1)}, f32[1,2,8,16,128]{4,3,2,1,0:T(8,128)}, u32[]{:S(2)}) %copy-start.1) | copy-done | bytes 131096
  2.5 0.0 copy-start.2
  2.5 0.8 %copy-done.2 = bf16[1,8,16,128]{3,2,1,0:T(8,128)(2,1)S(1)} copy-done((bf16[1,8,16,128]{3,2,1,0:T(8,128)(2,1)S(1)}, bf16[1,8,16,128]{3,2,1,0:T(8,128)(2,1)}, u32[]{:S(2)}) %copy-start.2) | copy-done | bytes 32792
  3.3 0.0 copy-start.3
  3.3 0.8 %copy-done.3 = bf16[1,8,16,128]{3,2,1,0:T(8,128)(2,1)S(1)} copy-done((bf16[1,8,16,128]{3,2,1,0:T(8,128)(2,1)S(1)}, bf16[1,8,16,128]{3,2,1,0:T(8,128)(2,1)}, u32[]{:S(2)}) %copy-start.3) | copy-done | bytes 32792
  4.0 0.0 copy-start.4
  4.0 0.8 %copy-done.4 = bf16[1,8,16,128]{3,2,1,0:T(8,128)(2,1)S(1)} copy-done((bf16[1,8,16,128]{3,2,1,0:T(8,128)(2,1)S(1)}, bf16[1,8,16,128]{3,2,1,0:T(8,128)(2,1)}, u32[]{:S(2)}) %copy-start.4) | copy-done | bytes 32792
  4.8 0.0 copy-start.5
  4.8 0.8 %copy-done.5 = bf16[1,8,16,128]{3,2,1,0:T(8,128)(2,1)S(1)} copy-done((bf16[1,8,16,128]{3,2,1,0:T(8,128)(2,1)S(1)}, bf16[1,8,16,128]{3,2,1,0:T(8,128)(2,1)}, u32[]{:S(2)}) %copy-start.5) | copy-done | bytes 32792
  5.5 21.0 %migrate.1 = f32[4,32,32]{2,1,0:T(8,128)S(1)} custom-call(s32[8]{0:T(128)S(1)} %copy-done.6, s32[32]{0:T(128)S(1)} %copy-done.7, s32[1,32]{1,0:T(1,128)S(1)} %bitcast.2, f32[1,32]{1,0:T(1,128)S(1)} %bitcast.3, f32[1,2,8,16,128]{4,3,2,1,0:T(8,128)S(1)} %copy-done, f32[1,2,8,16,128]{4,3,2,1,0:T(8,128)S(1)} %copy-done.1, bf16[1,8,16,128]{3,2,1,0:T(8,128)(2,1)S(1)} %copy-done.2, ...), custom_call_target="tpu_custom_call" | custom-call | tf_op jit(solution)/shard_map/migrate/pallas_call | solution.py:434
  26.6 0.6 %copy.12 = f32[4,32,32]{2,1,0:T(8,128)} copy(f32[4,32,32]{2,1,0:T(8,128)S(1)} %migrate.1) | data formatting | bytes 32768
Async XLA Ops:
  0.0 0.7 %copy-start.9 = (f32[32]{0:T(128)S(1)}, f32[32]{0:T(128)}, u32[]{:S(2)}) copy-start(f32[32]{0:T(128)} %param.19) | copy-start | bytes 388
  0.0 0.7 %copy-start.6 = (s32[8]{0:T(128)S(1)}, s32[8]{0:T(128)}, u32[]{:S(2)}) copy-start(s32[8]{0:T(128)} %anchor.1) | copy-start | bytes 100
  0.0 0.7 %copy-start.7 = (s32[32]{0:T(128)S(1)}, s32[32]{0:T(128)}, u32[]{:S(2)}) copy-start(s32[32]{0:T(128)} %slots.1) | copy-start | bytes 388
  0.0 0.7 %copy-start.8 = (s32[32]{0:T(128)S(1)}, s32[32]{0:T(128)}, u32[]{:S(2)}) copy-start(s32[32]{0:T(128)} %param.18) | copy-start | bytes 388
  0.7 0.9 %copy-start = (f32[1,2,8,16,128]{4,3,2,1,0:T(8,128)S(1)}, f32[1,2,8,16,128]{4,3,2,1,0:T(8,128)}, u32[]{:S(2)}) copy-start(f32[1,2,8,16,128]{4,3,2,1,0:T(8,128)} %prev_fields.1) | copy-start | bytes 393220
  1.6 0.9 %copy-start.1 = (f32[1,2,8,16,128]{4,3,2,1,0:T(8,128)S(1)}, f32[1,2,8,16,128]{4,3,2,1,0:T(8,128)}, u32[]{:S(2)}) copy-start(f32[1,2,8,16,128]{4,3,2,1,0:T(8,128)} %cur_fields.1) | copy-start | bytes 393220
  2.5 0.8 %copy-start.2 = (bf16[1,8,16,128]{3,2,1,0:T(8,128)(2,1)S(1)}, bf16[1,8,16,128]{3,2,1,0:T(8,128)(2,1)}, u32[]{:S(2)}) copy-start(bf16[1,8,16,128]{3,2,1,0:T(8,128)(2,1)} %speed_term.1) | copy-start | bytes 98308
  3.3 0.8 %copy-start.3 = (bf16[1,8,16,128]{3,2,1,0:T(8,128)(2,1)S(1)}, bf16[1,8,16,128]{3,2,1,0:T(8,128)(2,1)}, u32[]{:S(2)}) copy-start(bf16[1,8,16,128]{3,2,1,0:T(8,128)(2,1)} %epsilon.1) | copy-start | bytes 98308
  4.0 0.8 %copy-start.4 = (bf16[1,8,16,128]{3,2,1,0:T(8,128)(2,1)S(1)}, bf16[1,8,16,128]{3,2,1,0:T(8,128)(2,1)}, u32[]{:S(2)}) copy-start(bf16[1,8,16,128]{3,2,1,0:T(8,128)(2,1)} %tilt.1) | copy-start | bytes 98308
  4.8 0.8 %copy-start.5 = (bf16[1,8,16,128]{3,2,1,0:T(8,128)(2,1)S(1)}, bf16[1,8,16,128]{3,2,1,0:T(8,128)(2,1)}, u32[]{:S(2)}) copy-start(bf16[1,8,16,128]{3,2,1,0:T(8,128)(2,1)} %azimuth.1) | copy-start | bytes 98308

commit v2 on v1

--- a/solution.py
+++ b/solution.py
@@ -11,6 +11,7 @@
 IMB = 4
 WMAX = 4
 PAD = 8
+EARLY = 3
 MESH = pl.DeviceIdType.MESH
 SINE = (
     1.0,
@@ -66,7 +67,7 @@
     weights[6, layers] = 0.5 * (skew_x * axis_y)
 
 
-def negative_inverse(matrix):
+def sweep_rounds(matrix, result):
     size = matrix.shape[0]
     row_ids = lax.broadcasted_iota(jnp.int32, (size, size), 0)
     column_ids = lax.broadcasted_iota(jnp.int32, (size, size), 1)
@@ -88,7 +89,9 @@
             for k, row, column, scaled, inverse in parts:
                 edge = jnp.where(row_ids[:, :1] == k, -inverse, scaled)
                 matrix = jnp.where(column_ids == k, jnp.broadcast_to(edge, matrix.shape), matrix)
-    return matrix
+            if inner == WMAX - 1 and not active:
+                result[...] = matrix
+            yield
 
 
 def band_matrix(widths, damp):
@@ -109,10 +112,10 @@
 def kernel(
     shots,
     depths,
-    anchor,
-    slots,
-    widths,
-    damp,
+    anchor_in,
+    slots_in,
+    widths_in,
+    damp_in,
     prev_fields,
     cur_fields,
     speed_term,
@@ -120,6 +123,10 @@
     tilt,
     azimuth,
     out,
+    anchor,
+    slots,
+    widths,
+    damp,
     even,
     odd,
     raw,
@@ -144,7 +151,7 @@
     slab = speed_term.shape[1]
     span = speed_term.shape[2]
     lanes = speed_term.shape[3]
-    blocks = slots.shape[0]
+    blocks = slots_in.shape[0]
     half = slab // 2
     top = 3 * slab
     inner = pl.ds(PAD, span)
@@ -172,6 +179,10 @@
     local = [
         pltpu.make_async_copy(source(i, 0, slab), target(i, slab, 2 * slab), local_sem.at[i])
         for i in range(6)
+    ]
+    small = ((anchor_in, anchor), (slots_in, slots), (widths_in, widths), (damp_in, damp))
+    local += [
+        pltpu.make_async_copy(small[i][0], small[i][1], local_sem.at[6 + i]) for i in range(4)
     ]
     for copy in local:
         copy.start()
@@ -229,7 +240,9 @@
         copy.wait()
     for first in range(slab, 2 * slab, 2):
         store_weights(raw, weights, pl.ds(first, 2))
-    inverse[...] = negative_inverse(band_matrix(widths[...], damp[...]))
+    rounds = sweep_rounds(band_matrix(widths[...], damp[...]), inverse)
+    for _ in range(EARLY):
+        next(rounds, None)
     picture[...] = jnp.zeros(picture.shape, jnp.float32)
 
     lane_ids = lax.broadcasted_iota(jnp.int32, (2, span, lanes), 2)
@@ -278,6 +291,7 @@
             if own and slab <= z < 2 * slab:
                 picture[z - slab] += total[0] * total[1]
             below, here = here, above
+        next(rounds, None)
 
     def arrive(chunk):
         @pl.when(has_before)
@@ -309,6 +323,8 @@
         now, new = fields[(t - 1) % 2], fields[t % 2]
         advance(now, new, t, top - t, True)
 
+    for _ in rounds:
+        pass
     rows[...] = jnp.swapaxes(picture[...], 0, 1)
 
     my_anchor = anchor[shot]
@@ -428,16 +444,19 @@
     slab, span, lanes = speed_term.shape[1:]
     total = band_width.shape[0]
     f32 = jnp.float32
-    smem = pl.BlockSpec(memory_space=pltpu.SMEM)
     vmem = pl.BlockSpec(memory_space=pltpu.VMEM)
-    anywhere = pl.BlockSpec(memory_space=pl.ANY)
+    far = pl.BlockSpec(memory_space=pltpu.HBM)
     return pl.pallas_call(
         functools.partial(kernel, shots, depths),
         name="migrate",
         out_shape=jax.ShapeDtypeStruct((IMB, lanes // depths, total), f32),
-        in_specs=[smem, smem, vmem, vmem] + [anywhere] * 6,
+        in_specs=[far] * 10,
         out_specs=vmem,
         scratch_shapes=[
+            pltpu.SMEM(aperture_anchor.shape, jnp.int32),
+            pltpu.SMEM(slot_block.shape, jnp.int32),
+            pltpu.VMEM((1, total), jnp.int32),
+            pltpu.VMEM((1, total), f32),
             pltpu.VMEM((2, 3 * slab, span + 2 * PAD, lanes), f32),
             pltpu.VMEM((2, 3 * slab, span + 2 * PAD, lanes), f32),
             pltpu.VMEM((4, 3 * slab, span, lanes), speed_term.dtype),
@@ -449,7 +468,7 @@
             pltpu.VMEM((depths, slab, lanes), f32),
             pltpu.VMEM((total, lanes), f32),
             pltpu.VMEM((total, total), f32),
-            pltpu.SemaphoreType.DMA((6,)),
+            pltpu.SemaphoreType.DMA((10,)),
             pltpu.SemaphoreType.DMA((2, 2, 6)),
             pltpu.SemaphoreType.DMA((2, 2, 6)),
             pltpu.SemaphoreType.DMA((shots,)),
@@ -458,7 +477,7 @@
             pltpu.SemaphoreType.DMA((depths,)),
         ],
         compiler_params=pltpu.CompilerParams(
-            collective_id=0, has_side_effects=True, vmem_limit_bytes=48 * 1024 * 1024
+            collective_id=0, has_side_effects=True, vmem_limit_bytes=64 * 1024 * 1024
         ),
     )(
         aperture_anchor,

time: 27.6 us -> 23 us (0.83); the launches traced: 27.2 us -> 22.9 us
  local copies, waits for them, and re-layouts: 6.17 us -> 1.47 us
  Pallas kernels: 21 us -> 21.4 us
    unnamed x21 -> x1, local copies, waits for them, and re-layouts: 6.17 us -> 1.47 us
    pallas_call x1, Pallas kernels: 21 us -> 21.4 us  [shards(): pl.pallas_call(functools.partial(kernel, shots, depths), name='migrate',...]
where the time goes in v2:
time: 23 us; the launch traced here: 22.9 us
  Pallas kernels  21.4 us (93%)
  local copies, waits for them, and re-layouts  1.47 us (6%)
    pallas_call x1, Pallas kernels, shards(): pl.pallas_call(functools.partial(kernel, shots, depths), name='migrate',...  21.4 us
    unnamed x1, local copies, waits for them, and re-layouts  1.47 us

profile of v2, /device:TPU:0, one launch (start us, length us, event | category | flops | bytes accessed | tf_op | source)
XLA Modules:
  0.0 22.9 jit_solution(15713242772344553927)
XLA Ops:
  0.0 21.4 %migrate.1 = f32[4,32,32]{2,1,0:T(8,128)} custom-call(s32[8]{0:T(128)} %anchor_in.1, s32[32]{0:T(128)} %slots_in.1, s32[1,32]{1,0:T(1,128)} %bitcast.2, f32[1,32]{1,0:T(1,128)} %bitcast.3, f32[1,2,8,16,128]{4,3,2,1,0:T(8,128)} %prev_fields.1, f32[1,2,8,16,128]{4,3,2,1,0:T(8,128)} %cur_fields.1, bf16[1,8,16,128]{3,2,1,0:T(8,128)(2,1)} %speed_term.1, ...), custom_call_target="tpu_custom_call" | custom-call | tf_op jit(solution)/shard_map/migrate/pallas_call | solution.py:449
  21.4 1.5 %copy.12 = f32[4,32,32]{2,1,0:T(8,128)} copy(f32[4,32,32]{2,1,0:T(8,128)} %migrate.1) | data formatting | bytes 32768

commit v3 on v2

--- a/solution.py
+++ b/solution.py
@@ -305,13 +305,17 @@
                 halo(1, chunk, i).wait_recv()
 
     fields = (even, odd)
+    for t in range(1, half):
+        now, new = fields[(t - 1) % 2], fields[t % 2]
+        advance(now, new, slab + t, 2 * slab - t, True)
     arrive(0)
     for first in range(half, slab, 2):
         store_weights(raw, weights, pl.ds(first, 2))
         store_weights(raw, weights, pl.ds(2 * slab + first - half, 2))
     for t in range(1, half + 1):
         now, new = fields[(t - 1) % 2], fields[t % 2]
-        advance(now, new, half + t, top - half - t, True)
+        advance(now, new, half + t, slab + t, True)
+        advance(now, new, 2 * slab - t, top - half - t, True)
     arrive(1)
     for first, count in ((1, half - 1), (top - half, half - 1)):
         store_weights(raw, weights, pl.ds(first, count))
@@ -400,14 +404,12 @@
             slice_for(o).start()
     for o in range(1, depths):
         slice_for(o).wait_recv()
-    solved = lax.dot_general(
+    out[...] = -jnp.dot(
+        inverse[...],
         traces[...],
-        inverse[...],
-        (((0,), (0,)), ((), ())),
         precision=lax.Precision.HIGHEST,
         preferred_element_type=jnp.float32,
     )
-    out[...] = -solved[: IMB * share].reshape(out.shape)
 
     for chunk in range(2):
 
@@ -446,10 +448,10 @@
     f32 = jnp.float32
     vmem = pl.BlockSpec(memory_space=pltpu.VMEM)
     far = pl.BlockSpec(memory_space=pltpu.HBM)
-    return pl.pallas_call(
+    solved = pl.pallas_call(
         functools.partial(kernel, shots, depths),
         name="migrate",
-        out_shape=jax.ShapeDtypeStruct((IMB, lanes // depths, total), f32),
+        out_shape=jax.ShapeDtypeStruct((total, lanes), f32),
         in_specs=[far] * 10,
         out_specs=vmem,
         scratch_shapes=[
@@ -491,6 +493,8 @@
         tilt,
         azimuth,
     )
+    share = lanes // depths
+    return solved[:, : IMB * share].T.reshape(IMB, share, total)
 
 
 def solution(mesh):

time: 23 us -> 22.8 us (level)
  Pallas kernels: 21.4 us -> 21.1 us
    unnamed x1 -> x0, local copies, waits for them, and re-layouts: 1.47 us -> none
    reshape x0 -> x1, local copies, waits for them, and re-layouts: none -> 1.45 us  [shards(): return solved[:, :IMB * share].T.reshape(IMB, share, total)]
    pallas_call x1, Pallas kernels: 21.4 us -> 21.1 us  [shards(): pl.pallas_call(functools.partial(kernel, shots, depths), name='migrate',...]
where the time goes in v3:
time: 22.8 us; the launch traced here: 22.6 us
  Pallas kernels  21.1 us (93%)
  local copies, waits for them, and re-layouts  1.45 us (6%)
    pallas_call x1, Pallas kernels, shards(): pl.pallas_call(functools.partial(kernel, shots, depths), name='migrate',...  21.1 us
    reshape x1, local copies, waits for them, and re-layouts, shards(): return solved[:, :IMB * share].T.reshape(IMB, share, total)  1.45 us

profile of v3, /device:TPU:0, one launch (start us, length us, event | category | flops | bytes accessed | tf_op | source)
XLA Modules:
  0.0 22.6 jit_solution(14164384518988194142)
XLA Ops:
  0.0 21.1 %migrate.1 = f32[32,128]{1,0:T(8,128)} custom-call(s32[8]{0:T(128)} %anchor_in.1, s32[32]{0:T(128)} %slots_in.1, s32[1,32]{1,0:T(1,128)} %bitcast.5, f32[1,32]{1,0:T(1,128)} %bitcast.6, f32[1,2,8,16,128]{4,3,2,1,0:T(8,128)} %prev_fields.1, f32[1,2,8,16,128]{4,3,2,1,0:T(8,128)} %cur_fields.1, bf16[1,8,16,128]{3,2,1,0:T(8,128)(2,1)} %speed_term.1, ...), custom_call_target="tpu_custom_call" | custom-call | tf_op jit(solution)/shard_map/migrate/pallas_call | solution.py:451
  21.2 1.4 %copy.12 = f32[128,32]{1,0:T(8,128)} copy(f32[128,32]{0,1:T(8,128)} %bitcast.4) | data formatting | bytes 32768 | tf_op jit(solution)/shard_map/reshape | solution.py:497

commit v4 on v3

--- a/solution.py
+++ b/solution.py
@@ -127,8 +127,8 @@
     slots,
     widths,
     damp,
-    even,
-    odd,
+    state,
+    stage,
     raw,
     weights,
     picture,
@@ -155,6 +155,7 @@
     half = slab // 2
     top = 3 * slab
     inner = pl.ds(PAD, span)
+    even, odd = state.at[0], state.at[1]
 
     barrier = pltpu.get_barrier_semaphore()
     for o in range(1, depths):
@@ -166,30 +167,23 @@
 
     params = (speed_term, epsilon, tilt, azimuth)
 
-    def source(i, first, last):
-        if i < 2:
-            return (cur_fields, prev_fields)[i].at[0, :, pl.ds(first, last - first)]
-        return params[i - 2].at[0, pl.ds(first, last - first)]
-
-    def target(i, first, last):
-        if i < 2:
-            return (even, odd)[i].at[:, pl.ds(first, last - first), inner]
-        return raw.at[i - 2, pl.ds(first, last - first)]
-
+    own = pl.ds(slab, slab)
+    moves = [(cur_fields.at[0], stage.at[0]), (prev_fields.at[0], stage.at[1])]
+    moves += [(params[i].at[0], raw.at[i, own]) for i in range(4)]
+    moves += [(cur_fields.at[0], even.at[:, own, inner]), (prev_fields.at[0], odd.at[:, own, inner])]
+    moves += [(anchor_in, anchor), (slots_in, slots), (widths_in, widths), (damp_in, damp)]
     local = [
-        pltpu.make_async_copy(source(i, 0, slab), target(i, slab, 2 * slab), local_sem.at[i])
-        for i in range(6)
-    ]
-    small = ((anchor_in, anchor), (slots_in, slots), (widths_in, widths), (damp_in, damp))
-    local += [
-        pltpu.make_async_copy(small[i][0], small[i][1], local_sem.at[6 + i]) for i in range(4)
+        pltpu.make_async_copy(first, second, local_sem.at[i])
+        for i, (first, second) in enumerate(moves)
     ]
     for copy in local:
         copy.start()
     pl.semaphore_wait(barrier, depths + shots - 2)
+    for copy in local[:6]:
+        copy.wait()
 
     def halo(side, chunk, i):
-        cut = 0 if i == 0 else 1
+        cut = i
         if side == 0:
             first, last = ((half, slab), (cut, half))[chunk]
             place = first
@@ -198,9 +192,16 @@
             first, last = ((0, half), (half, slab - cut))[chunk]
             place = 2 * slab + first
             step = -1
+        count = last - first
+        if i == 0:
+            here = stage.at[:, :, pl.ds(first, count)]
+            there = state.at[:, :, pl.ds(place, count), inner]
+        else:
+            here = raw.at[:, pl.ds(slab + first, count)]
+            there = raw.at[:, pl.ds(place, count)]
         return pltpu.make_async_remote_copy(
-            src_ref=source(i, first, last),
-            dst_ref=target(i, place, place + last - first),
+            src_ref=here,
+            dst_ref=there,
             send_sem=halo_send.at[side, chunk, i],
             recv_sem=halo_recv.at[side, chunk, i],
             device_id={"depth": lax.rem(depth + step + depths, depths)},
@@ -213,12 +214,12 @@
 
         @pl.when(has_next)
         def _():
-            for i in range(6):
+            for i in range(2):
                 halo(0, chunk, i).start()
 
         @pl.when(has_before)
         def _():
-            for i in range(6):
+            for i in range(2):
                 halo(1, chunk, i).start()
 
     margin = jnp.zeros((2, top, PAD, lanes), jnp.float32)
@@ -236,7 +237,7 @@
     pl.when(jnp.logical_not(has_before))(lambda: clear(0))
     pl.when(jnp.logical_not(has_next))(lambda: clear(2 * slab))
 
-    for copy in local:
+    for copy in local[6:]:
         copy.wait()
     for first in range(slab, 2 * slab, 2):
         store_weights(raw, weights, pl.ds(first, 2))
@@ -296,12 +297,12 @@
     def arrive(chunk):
         @pl.when(has_before)
         def _():
-            for i in range(6):
+            for i in range(2):
                 halo(0, chunk, i).wait_recv()
 
         @pl.when(has_next)
         def _():
-            for i in range(6):
+            for i in range(2):
                 halo(1, chunk, i).wait_recv()
 
     fields = (even, odd)
@@ -415,12 +416,12 @@
 
         @pl.when(has_next)
         def _():
-            for i in range(6):
+            for i in range(2):
                 halo(0, chunk, i).wait_send()
 
         @pl.when(has_before)
         def _():
-            for i in range(6):
+            for i in range(2):
                 halo(1, chunk, i).wait_send()
 
     for o in range(1, shots):
@@ -459,8 +460,8 @@
             pltpu.SMEM(slot_block.shape, jnp.int32),
             pltpu.VMEM((1, total), jnp.int32),
             pltpu.VMEM((1, total), f32),
-            pltpu.VMEM((2, 3 * slab, span + 2 * PAD, lanes), f32),
-            pltpu.VMEM((2, 3 * slab, span + 2 * PAD, lanes), f32),
+            pltpu.VMEM((2, 2, 3 * slab, span + 2 * PAD, lanes), f32),
+            pltpu.VMEM((2, 2, slab, span, lanes), f32),
             pltpu.VMEM((4, 3 * slab, span, lanes), speed_term.dtype),
             pltpu.VMEM((7, 3 * slab, span, lanes), f32),
             pltpu.VMEM((slab, span, lanes), f32),
@@ -470,9 +471,9 @@
             pltpu.VMEM((depths, slab, lanes), f32),
             pltpu.VMEM((total, lanes), f32),
             pltpu.VMEM((total, total), f32),
-            pltpu.SemaphoreType.DMA((10,)),
-            pltpu.SemaphoreType.DMA((2, 2, 6)),
-            pltpu.SemaphoreType.DMA((2, 2, 6)),
+            pltpu.SemaphoreType.DMA((12,)),
+            pltpu.SemaphoreType.DMA((2, 2, 2)),
+            pltpu.SemaphoreType.DMA((2, 2, 2)),
             pltpu.SemaphoreType.DMA((shots,)),
             pltpu.SemaphoreType.DMA((shots,)),
             pltpu.SemaphoreType.DMA((depths,)),

time: 22.8 us -> 22.5 us (0.987)
  Pallas kernels: 21.1 us -> 20.8 us
    pallas_call x1, Pallas kernels: 21.1 us -> 20.8 us  [shards(): pl.pallas_call(functools.partial(kernel, shots, depths), name='migrate',...]
where the time goes in v4:
time: 22.5 us; the launch traced here: 22.3 us
  Pallas kernels  20.8 us (92%)
  local copies, waits for them, and re-layouts  1.45 us (6%)
    pallas_call x1, Pallas kernels, shards(): pl.pallas_call(functools.partial(kernel, shots, depths), name='migrate',...  20.8 us
    reshape x1, local copies, waits for them, and re-layouts, shards(): return solved[:, :IMB * share].T.reshape(IMB, share, total)  1.45 us

profile of v4, /device:TPU:0, one launch (start us, length us, event | category | flops | bytes accessed | tf_op | source)
XLA Modules:
  0.0 22.3 jit_solution(3270764846369821417)
XLA Ops:
  0.0 20.8 %migrate.1 = f32[32,128]{1,0:T(8,128)} custom-call(s32[8]{0:T(128)} %anchor_in.1, s32[32]{0:T(128)} %slots_in.1, s32[1,32]{1,0:T(1,128)} %bitcast.5, f32[1,32]{1,0:T(1,128)} %bitcast.6, f32[1,2,8,16,128]{4,3,2,1,0:T(8,128)} %prev_fields.1, f32[1,2,8,16,128]{4,3,2,1,0:T(8,128)} %cur_fields.1, bf16[1,8,16,128]{3,2,1,0:T(8,128)(2,1)} %speed_term.1, ...), custom_call_target="tpu_custom_call" | custom-call | tf_op jit(solution)/shard_map/migrate/pallas_call | solution.py:452
  20.8 1.4 %copy.12 = f32[128,32]{1,0:T(8,128)} copy(f32[128,32]{0,1:T(8,128)} %bitcast.4) | data formatting | bytes 32768 | tf_op jit(solution)/shard_map/reshape | solution.py:498

commit v5 on v4

--- a/solution.py
+++ b/solution.py
@@ -11,7 +11,8 @@
 IMB = 4
 WMAX = 4
 PAD = 8
-EARLY = 3
+EARLY = 8
+LATER = 5
 MESH = pl.DeviceIdType.MESH
 SINE = (
     1.0,
@@ -292,7 +293,6 @@
             if own and slab <= z < 2 * slab:
                 picture[z - slab] += total[0] * total[1]
             below, here = here, above
-        next(rounds, None)
 
     def arrive(chunk):
         @pl.when(has_before)
@@ -328,8 +328,6 @@
         now, new = fields[(t - 1) % 2], fields[t % 2]
         advance(now, new, t, top - t, True)
 
-    for _ in rounds:
-        pass
     rows[...] = jnp.swapaxes(picture[...], 0, 1)
 
     my_anchor = anchor[shot]
@@ -364,6 +362,8 @@
         if o > 0:
             parcel(o).start()
 
+    for _ in range(LATER):
+        next(rounds, None)
     owned = [jnp.zeros((slab, lanes), jnp.float32) for _ in range(IMB)]
     held = [slots[shot * IMB + j] for j in range(IMB)]
     for o in range(shots):
@@ -403,6 +403,8 @@
         else:
             packed[o] = block
             slice_for(o).start()
+    for _ in rounds:
+        pass
     for o in range(1, depths):
         slice_for(o).wait_recv()
     out[...] = -jnp.dot(

time: 22.5 us -> 22.6 us (level)
  no operation moved by 1% of the time
where the time goes in v5:
time: 22.6 us; the launch traced here: 22.3 us
  Pallas kernels  20.9 us (92%)
  local copies, waits for them, and re-layouts  1.45 us (6%)
    pallas_call x1, Pallas kernels, shards(): pl.pallas_call(functools.partial(kernel, shots, depths), name='migrate',...  20.9 us
    reshape x1, local copies, waits for them, and re-layouts, shards(): return solved[:, :IMB * share].T.reshape(IMB, share, total)  1.45 us

profile of v5, /device:TPU:0, one launch (start us, length us, event | category | flops | bytes accessed | tf_op | source)
XLA Modules:
  0.0 22.3 jit_solution(5709716519723422122)
XLA Ops:
  0.0 20.9 %migrate.1 = f32[32,128]{1,0:T(8,128)} custom-call(s32[8]{0:T(128)} %anchor_in.1, s32[32]{0:T(128)} %slots_in.1, s32[1,32]{1,0:T(1,128)} %bitcast.5, f32[1,32]{1,0:T(1,128)} %bitcast.6, f32[1,2,8,16,128]{4,3,2,1,0:T(8,128)} %prev_fields.1, f32[1,2,8,16,128]{4,3,2,1,0:T(8,128)} %cur_fields.1, bf16[1,8,16,128]{3,2,1,0:T(8,128)(2,1)} %speed_term.1, ...), custom_call_target="tpu_custom_call" | custom-call | tf_op jit(solution)/shard_map/migrate/pallas_call | solution.py:454
  20.9 1.4 %copy.12 = f32[128,32]{1,0:T(8,128)} copy(f32[128,32]{0,1:T(8,128)} %bitcast.4) | data formatting | bytes 32768 | tf_op jit(solution)/shard_map/reshape | solution.py:500
